TPU v7x, 32 devices: a whole 2x2x4 slice. The times are simulated.
32 devices in a mesh: row: 4 (over x, core), col: 8 (over z, y).
Axes of the slice: x: 2, y: 2, z: 4, core: 2. Of those that a mesh axis runs over, the one named last changes fastest.
Arguments:
- features: bfloat16 [2048, 8, 128], P('row', 'col'), may hold values from -6 to 6
- first_weight: bfloat16 [128, 256], replicated, may hold values from -0.5 to 0.5
- first_bias: float32 [256], replicated, may hold values from -4 to 4
- second_weight: bfloat16 [256, 256], replicated, may hold values from -0.375 to 0.375
- second_bias: float32 [256], replicated, may hold values from -4 to 4
- tile_values: bfloat16 [128, 64, 128, 128], P('row', 'col'), may hold values from -0.09375 to 0.09375
- tile_columns: int32 [128, 64], P('row', 'col'), may hold values from 0 to 15
- tile_counts: int32 [128, 8], P('row', 'col'), may hold values from 1 to 8
Outputs:
- output: bfloat16 [16384, 256], P(('row', 'col'))
Inputs may be any that keep to these rules, and one draw needn't show every extreme that they name: `tile_columns`: entries of slots at or beyond their block row's count are ignored.
All inputs are finite; a program needn't handle non-finite values.
Results may differ from a plain program's by a relative error of at most 0.015.
Values may be sent and summed in bfloat16 or wider, within the bound.
A program may use at most 128 MiB of HBM per device.

v0:
```python
import jax
import jax.numpy as jnp
from jax import lax
from jax.sharding import PartitionSpec as P


def combine_rows(panels, tile_values, tile_columns, tile_counts):
    rows_dev, slot_count, tile_size, _ = tile_values.shape
    hidden_width = panels.shape[-1]
    groups = rows_dev // 8

    def one_group(inputs):
        values, columns, counts = inputs
        fetched = jnp.take(panels, columns, axis=0)
        usable = jnp.arange(slot_count, dtype=jnp.int32)[None, :] < counts
        fetched = jnp.where(usable[:, :, None, None], fetched, jnp.zeros((), jnp.bfloat16))
        return jnp.einsum("rsik,rskf->rif", values, fetched, preferred_element_type=jnp.float32)

    results = lax.map(
        one_group,
        (
            tile_values.reshape(groups, 8, slot_count, tile_size, tile_size),
            tile_columns.reshape(groups, 8, slot_count),
            tile_counts.reshape(groups, 8, 1),
        ),
    )
    return results.reshape(rows_dev * tile_size, hidden_width)


def local(
    features,
    first_weight,
    first_bias,
    second_weight,
    second_bias,
    tile_values,
    tile_columns,
    tile_counts,
):
    nodes_dev = features.shape[0]
    feature_width = features.shape[2]
    hidden_width = first_weight.shape[1]
    tile_size = tile_values.shape[-1]
    col_devices = lax.axis_size("col")
    scaled = jnp.dot(
        features.reshape(nodes_dev, feature_width), first_weight, preferred_element_type=jnp.float32
    ).astype(jnp.bfloat16)
    panels = lax.all_gather(scaled.reshape(nodes_dev, 1, hidden_width), "row", axis=0, tiled=True)
    panels = panels.reshape(-1, tile_size, hidden_width)
    partial_value = combine_rows(panels, tile_values, tile_columns, tile_counts)
    summed = lax.psum_scatter(
        partial_value.astype(jnp.bfloat16), "col", scatter_dimension=0, tiled=True
    ).astype(jnp.float32)
    hidden = jnp.maximum(summed + first_bias, 0.0).astype(jnp.bfloat16)
    hidden = lax.all_to_all(
        hidden.reshape(1, nodes_dev // col_devices, col_devices, hidden_width),
        "col",
        split_axis=2,
        concat_axis=0,
        tiled=True,
    )
    hidden = hidden.reshape(nodes_dev, hidden_width)
    second = jnp.dot(hidden, second_weight, preferred_element_type=jnp.float32).astype(jnp.bfloat16)
    panels = lax.all_gather(second.reshape(nodes_dev, 1, hidden_width), "row", axis=0, tiled=True)
    panels = panels.reshape(-1, tile_size, hidden_width)
    partial_value = combine_rows(panels, tile_values, tile_columns, tile_counts)
    summed = lax.psum_scatter(
        partial_value.astype(jnp.bfloat16), "col", scatter_dimension=0, tiled=True
    ).astype(jnp.float32)
    return jnp.maximum(summed + second_bias, 0.0).astype(jnp.bfloat16)


def solution(mesh):
    return jax.shard_map(
        local,
        mesh=mesh,
        in_specs=(
            P("row", "col", None),
            P(),
            P(),
            P(),
            P(),
            P("row", "col", None, None),
            P("row", "col"),
            P("row", "col"),
        ),
        out_specs=P(("row", "col"), None),
        check_vma=False,
    )
```

profile of v0, /device:TPU:0, one launch (start us, length us, event | category | flops | bytes accessed | tf_op | source)
XLA Modules:
  0.0 268.0 jit_solution(13620643965749158856)
XLA Ops:
  6.5 0.9 copy-done
  7.4 1.8 convolution_convert_fusion.1
  9.8 1.2 reduce.3
  11.1 0.8 copy.19
  11.9 16.9 %all-gather.5.cloned.1.call-done = bf16[2048,256]{1,0:T(8,128)(2,1)} async-done(((bf16[512,256]{1,0:T(8,128)(2,1)}), bf16[2048,256]{1,0:T(8,128)(2,1)}) %all-gather.5.cloned.1.call-update) | async-done | bytes 1048592 | tf_op jit(solution)/shard_map/all_gather | solution.py:48
  29.0 31.3 %while.20 = (s32[]{:T(128)}, bf16[4,8,128,256]{3,2,1,0:T(8,128)(2,1)S(1)}, bf16[4,8,8,128,128]{4,3,2,1,0:T(8,128)(2,1)}, s32[4,8,1]{1,2,0:T(1,128)S(1)}, s32[4,8...) while((s32[]{:T(128)}, bf16[4,8,128,256]{3,2,1,0:T(8,128)(2,1)S(1)}, ...), condition=%wide.region_1.3_spmd, body=%wide.region_0.2_spmd.sunk | while | flops 541066688 | bytes 15737653 | solution.py:19
  29.2 4.0 %gather_fusion = bf16[64,128,256]{2,1,0:T(8,128)(2,1)} fusion(bf16[16,128,256]{2,1,0:T(8,128)(2,1)} %get-tuple-element.255, s32[1024]{0:T(1024)S(1)} %pad_clamp_fusion.4), kind=kCustom, calls=%fused_computation.clone.clone.1 | custom fusion | bytes 8388864 | tf_op jit(solution)/shard_map/while/body/eval_jaxpr/jit(_take)/gather | solution.py:14
  33.2 3.6 %fusion.47 = bf16[4,8,128,256]{3,2,1,0:T(8,128)(2,1)S(1)} fusion(bf16[4,8,128,256]{3,2,1,0:T(8,128)(2,1)S(1)} %get-tuple-element.244, s32[]{:T(128)} %get-tuple-element.243, bf16[8,8,128,256]{3,2,1,0:T(8,128)(2,1)} %bitcast.78, pred[8,8]{1,0:T(8,128)(4,1)S(1)} %get-tuple-element.225, pred[8,8]{1,0:T(8,128)(4,1)S(1)} %get-tuple-element.226, ...), kind=kOutput, calls=%fused_computation.11.clone.1 | convolution fusion | flops 541065216 | bytes 7343104 | tf_op jit(solution)/shard_map/while/body/eval_jaxpr/rsik,rskf->rif/dot_general | solution.py:17
  37.1 4.0 %gather_fusion = bf16[64,128,256]{2,1,0:T(8,128)(2,1)} fusion(bf16[16,128,256]{2,1,0:T(8,128)(2,1)} %get-tuple-element.255, s32[1024]{0:T(1024)S(1)} %pad_clamp_fusion.4), kind=kCustom, calls=%fused_computation.clone.clone.1 | custom fusion | bytes 8388864 | tf_op jit(solution)/shard_map/while/body/eval_jaxpr/jit(_take)/gather | solution.py:14
  41.0 3.6 %fusion.47 = bf16[4,8,128,256]{3,2,1,0:T(8,128)(2,1)S(1)} fusion(bf16[4,8,128,256]{3,2,1,0:T(8,128)(2,1)S(1)} %get-tuple-element.244, s32[]{:T(128)} %get-tuple-element.243, bf16[8,8,128,256]{3,2,1,0:T(8,128)(2,1)} %bitcast.78, pred[8,8]{1,0:T(8,128)(4,1)S(1)} %get-tuple-element.225, pred[8,8]{1,0:T(8,128)(4,1)S(1)} %get-tuple-element.226, ...), kind=kOutput, calls=%fused_computation.11.clone.1 | convolution fusion | flops 541065216 | bytes 7343104 | tf_op jit(solution)/shard_map/while/body/eval_jaxpr/rsik,rskf->rif/dot_general | solution.py:17
  44.9 4.0 %gather_fusion = bf16[64,128,256]{2,1,0:T(8,128)(2,1)} fusion(bf16[16,128,256]{2,1,0:T(8,128)(2,1)} %get-tuple-element.255, s32[1024]{0:T(1024)S(1)} %pad_clamp_fusion.4), kind=kCustom, calls=%fused_computation.clone.clone.1 | custom fusion | bytes 8388864 | tf_op jit(solution)/shard_map/while/body/eval_jaxpr/jit(_take)/gather | solution.py:14
  48.9 3.6 %fusion.47 = bf16[4,8,128,256]{3,2,1,0:T(8,128)(2,1)S(1)} fusion(bf16[4,8,128,256]{3,2,1,0:T(8,128)(2,1)S(1)} %get-tuple-element.244, s32[]{:T(128)} %get-tuple-element.243, bf16[8,8,128,256]{3,2,1,0:T(8,128)(2,1)} %bitcast.78, pred[8,8]{1,0:T(8,128)(4,1)S(1)} %get-tuple-element.225, pred[8,8]{1,0:T(8,128)(4,1)S(1)} %get-tuple-element.226, ...), kind=kOutput, calls=%fused_computation.11.clone.1 | convolution fusion | flops 541065216 | bytes 7343104 | tf_op jit(solution)/shard_map/while/body/eval_jaxpr/rsik,rskf->rif/dot_general | solution.py:17
  52.7 4.0 %gather_fusion = bf16[64,128,256]{2,1,0:T(8,128)(2,1)} fusion(bf16[16,128,256]{2,1,0:T(8,128)(2,1)} %get-tuple-element.255, s32[1024]{0:T(1024)S(1)} %pad_clamp_fusion.4), kind=kCustom, calls=%fused_computation.clone.clone.1 | custom fusion | bytes 8388864 | tf_op jit(solution)/shard_map/while/body/eval_jaxpr/jit(_take)/gather | solution.py:14
  56.7 3.6 %fusion.47 = bf16[4,8,128,256]{3,2,1,0:T(8,128)(2,1)S(1)} fusion(bf16[4,8,128,256]{3,2,1,0:T(8,128)(2,1)S(1)} %get-tuple-element.244, s32[]{:T(128)} %get-tuple-element.243, bf16[8,8,128,256]{3,2,1,0:T(8,128)(2,1)} %bitcast.78, pred[8,8]{1,0:T(8,128)(4,1)S(1)} %get-tuple-element.225, pred[8,8]{1,0:T(8,128)(4,1)S(1)} %get-tuple-element.226, ...), kind=kOutput, calls=%fused_computation.11.clone.1 | convolution fusion | flops 541065216 | bytes 7343104 | tf_op jit(solution)/shard_map/while/body/eval_jaxpr/rsik,rskf->rif/dot_general | solution.py:17
  60.3 1.3 copy-done.2
  61.7 68.1 %reduce-scatter.3.cloned.1.call-done = bf16[512,256]{1,0:T(8,128)(2,1)} async-done(((bf16[4096,256]{1,0:T(8,128)(2,1)}), bf16[512,256]{1,0:T(8,128)(2,1)}) %reduce-scatter.3.cloned.1.call-update) | async-done | bytes 262160 | tf_op jit(solution)/shard_map/reduce_scatter | solution.py:51
  129.8 1.0 fusion.34
  130.9 11.6 %all_to_all.15 = bf16[1,64,8,256]{3,1,0,2:T(8,128)(2,1)S(1)} all-to-all(bf16[1,64,8,256]{3,1,0,2:T(8,128)(2,1)S(1)} %copy.21), channel_id=1, replica_groups=mesh['row'=4,'col'=8] {'col'}, dimensions={2} | all-to-all | bytes 524288 | tf_op jit(solution)/shard_map/all_to_all | solution.py:55
  142.5 0.9 convolution_convert_fusion
  143.5 15.3 %all-gather.7.cloned.1.call-done = bf16[2048,256]{1,0:T(8,128)(2,1)} async-done(((bf16[512,256]{1,0:T(8,128)(2,1)}), bf16[2048,256]{1,0:T(8,128)(2,1)}) %all-gather.7.cloned.1.call-update) | async-done | bytes 1048592 | tf_op jit(solution)/shard_map/all_gather | solution.py:64
  159.0 31.3 %while.21 = (s32[]{:T(128)}, bf16[4,8,128,256]{3,2,1,0:T(8,128)(2,1)S(1)}, bf16[4,8,8,128,128]{4,3,2,1,0:T(8,128)(2,1)}, s32[4,8,1]{1,2,0:T(1,128)S(1)}, s32[4,8...) while((s32[]{:T(128)}, bf16[4,8,128,256]{3,2,1,0:T(8,128)(2,1)S(1)}, ...), condition=%wide.region_4.6_spmd, body=%wide.region_3.5_spmd.sunk | while | flops 541066688 | bytes 15737653 | solution.py:19
  159.2 4.0 %gather_fusion.1 = bf16[64,128,256]{2,1,0:T(8,128)(2,1)} fusion(bf16[16,128,256]{2,1,0:T(8,128)(2,1)} %get-tuple-element.276, s32[1024]{0:T(1024)S(1)} %pad_clamp_fusion.5), kind=kCustom, calls=%fused_computation.1.clone.clone.1 | custom fusion | bytes 8388864 | tf_op jit(solution)/shard_map/while/body/eval_jaxpr/jit(_take)/gather | solution.py:14
  163.2 3.6 %fusion.50 = bf16[4,8,128,256]{3,2,1,0:T(8,128)(2,1)S(1)} fusion(bf16[4,8,128,256]{3,2,1,0:T(8,128)(2,1)S(1)} %get-tuple-element.265, s32[]{:T(128)} %get-tuple-element.264, bf16[8,8,128,256]{3,2,1,0:T(8,128)(2,1)} %bitcast.79, pred[8,8]{1,0:T(8,128)(4,1)S(1)} %get-tuple-element.234, pred[8,8]{1,0:T(8,128)(4,1)S(1)} %get-tuple-element.235, ...), kind=kOutput, calls=%fused_computation.30.clone.1 | convolution fusion | flops 541065216 | bytes 7343104 | tf_op jit(solution)/shard_map/while/body/eval_jaxpr/rsik,rskf->rif/dot_general | solution.py:17
  167.0 4.0 %gather_fusion.1 = bf16[64,128,256]{2,1,0:T(8,128)(2,1)} fusion(bf16[16,128,256]{2,1,0:T(8,128)(2,1)} %get-tuple-element.276, s32[1024]{0:T(1024)S(1)} %pad_clamp_fusion.5), kind=kCustom, calls=%fused_computation.1.clone.clone.1 | custom fusion | bytes 8388864 | tf_op jit(solution)/shard_map/while/body/eval_jaxpr/jit(_take)/gather | solution.py:14
  171.0 3.6 %fusion.50 = bf16[4,8,128,256]{3,2,1,0:T(8,128)(2,1)S(1)} fusion(bf16[4,8,128,256]{3,2,1,0:T(8,128)(2,1)S(1)} %get-tuple-element.265, s32[]{:T(128)} %get-tuple-element.264, bf16[8,8,128,256]{3,2,1,0:T(8,128)(2,1)} %bitcast.79, pred[8,8]{1,0:T(8,128)(4,1)S(1)} %get-tuple-element.234, pred[8,8]{1,0:T(8,128)(4,1)S(1)} %get-tuple-element.235, ...), kind=kOutput, calls=%fused_computation.30.clone.1 | convolution fusion | flops 541065216 | bytes 7343104 | tf_op jit(solution)/shard_map/while/body/eval_jaxpr/rsik,rskf->rif/dot_general | solution.py:17
  174.9 4.0 %gather_fusion.1 = bf16[64,128,256]{2,1,0:T(8,128)(2,1)} fusion(bf16[16,128,256]{2,1,0:T(8,128)(2,1)} %get-tuple-element.276, s32[1024]{0:T(1024)S(1)} %pad_clamp_fusion.5), kind=kCustom, calls=%fused_computation.1.clone.clone.1 | custom fusion | bytes 8388864 | tf_op jit(solution)/shard_map/while/body/eval_jaxpr/jit(_take)/gather | solution.py:14
  178.8 3.6 %fusion.50 = bf16[4,8,128,256]{3,2,1,0:T(8,128)(2,1)S(1)} fusion(bf16[4,8,128,256]{3,2,1,0:T(8,128)(2,1)S(1)} %get-tuple-element.265, s32[]{:T(128)} %get-tuple-element.264, bf16[8,8,128,256]{3,2,1,0:T(8,128)(2,1)} %bitcast.79, pred[8,8]{1,0:T(8,128)(4,1)S(1)} %get-tuple-element.234, pred[8,8]{1,0:T(8,128)(4,1)S(1)} %get-tuple-element.235, ...), kind=kOutput, calls=%fused_computation.30.clone.1 | convolution fusion | flops 541065216 | bytes 7343104 | tf_op jit(solution)/shard_map/while/body/eval_jaxpr/rsik,rskf->rif/dot_general | solution.py:17
  182.7 4.0 %gather_fusion.1 = bf16[64,128,256]{2,1,0:T(8,128)(2,1)} fusion(bf16[16,128,256]{2,1,0:T(8,128)(2,1)} %get-tuple-element.276, s32[1024]{0:T(1024)S(1)} %pad_clamp_fusion.5), kind=kCustom, calls=%fused_computation.1.clone.clone.1 | custom fusion | bytes 8388864 | tf_op jit(solution)/shard_map/while/body/eval_jaxpr/jit(_take)/gather | solution.py:14
  186.7 3.6 %fusion.50 = bf16[4,8,128,256]{3,2,1,0:T(8,128)(2,1)S(1)} fusion(bf16[4,8,128,256]{3,2,1,0:T(8,128)(2,1)S(1)} %get-tuple-element.265, s32[]{:T(128)} %get-tuple-element.264, bf16[8,8,128,256]{3,2,1,0:T(8,128)(2,1)} %bitcast.79, pred[8,8]{1,0:T(8,128)(4,1)S(1)} %get-tuple-element.234, pred[8,8]{1,0:T(8,128)(4,1)S(1)} %get-tuple-element.235, ...), kind=kOutput, calls=%fused_computation.30.clone.1 | convolution fusion | flops 541065216 | bytes 7343104 | tf_op jit(solution)/shard_map/while/body/eval_jaxpr/rsik,rskf->rif/dot_general | solution.py:17
  190.3 1.3 copy-done.1
  191.7 68.1 %reduce-scatter.5.cloned.1.call-done = bf16[512,256]{1,0:T(8,128)(2,1)} async-done(((bf16[4096,256]{1,0:T(8,128)(2,1)}), bf16[512,256]{1,0:T(8,128)(2,1)}) %reduce-scatter.5.cloned.1.call-update) | async-done | bytes 262160 | tf_op jit(solution)/shard_map/reduce_scatter | solution.py:67
  259.7 1.7 maximum_convert_fusion
  (54 shorter events, 2.7 us)
Async XLA Ops:
  6.5 0.9 copy-start
  6.5 22.2 %all-gather.5.cloned.1.call-start = ((), (), s32[]{:S(2)}) async-start(), calls=%async_computation.5 | async-start | bytes 1310720 | tf_op jit(solution)/shard_map/all_gather | solution.py:48
  9.2 120.6 %reduce-scatter.3.cloned.1.call-start = ((), (), s32[]{:S(2)}) async-start(), calls=%async_computation.3 | async-start | bytes 2359296 | tf_op jit(solution)/shard_map/reduce_scatter | solution.py:51
  29.0 100.8 %copy-start.4 = (f32[256]{0:T(256)S(1)}, f32[256]{0:T(256)}, u32[]{:S(2)}) copy-start(f32[256]{0:T(256)} %param.16) | copy-start | bytes 3076
  29.0 113.4 %copy-start.3 = (bf16[256,256]{1,0:T(8,128)(2,1)S(1)}, bf16[256,256]{1,0:T(8,128)(2,1)}, u32[]{:S(2)}) copy-start(bf16[256,256]{1,0:T(8,128)(2,1)} %param.17) | copy-start | bytes 393220
  60.3 1.3 copy-start.2
  61.7 97.1 %all-gather.7.cloned.1.call-start = ((), (), s32[]{:S(2)}) async-start(), calls=%async_computation.6 | async-start | bytes 1310720 | tf_op jit(solution)/shard_map/all_gather | solution.py:64
  143.4 116.3 %reduce-scatter.5.cloned.1.call-start = ((), (), s32[]{:S(2)}) async-start(), calls=%async_computation.4 | async-start | bytes 2359296 | tf_op jit(solution)/shard_map/reduce_scatter | solution.py:67
  159.0 100.7 %copy-start.5 = (f32[256]{0:T(256)S(1)}, f32[256]{0:T(256)}, u32[]{:S(2)}) copy-start(f32[256]{0:T(256)} %param.18) | copy-start | bytes 3076
  190.3 1.3 copy-start.1
Sparse Core Ops, SparseCore 0:
  9.3 19.4 all-gather.4
  61.8 67.9 reduce-scatter.2
  143.5 15.2 all-gather.6
  191.8 67.8 reduce-scatter.4
where the time goes:
time: 269 us; the launch traced here: 268 us
  waiting for transfers between devices  168 us (62%)
  local copies, waits for them, and re-layouts  38 us (14%)
  matrix products  31.7 us (12%)
  between operations  13.2 us (5%)
  blocking collectives  11.6 us (4%)
  other arithmetic  4.64 us (2%)
    reduce_scatter x2, waiting for transfers between devices, local(): lax.psum_scatter(partial_value.astype(jnp.bfloat16), 'col', scatter_dimen...  136 us
    gather x8, local copies, waits for them, and re-layouts, one_group(): fetched = jnp.take(panels, columns, axis=0)  31.9 us
    dot_general x8, matrix products, one_group(): jnp.einsum('rsik,rskf->rif', values, fetched, preferred_element_type=jnp....  29 us
    all_gather x1, waiting for transfers between devices, local(): lax.all_gather(scaled.reshape(nodes_dev, 1, hidden_width), 'row', axis=0,...  16.9 us
    all_gather x1, waiting for transfers between devices, local(): lax.all_gather(second.reshape(nodes_dev, 1, hidden_width), 'row', axis=0,...  15.3 us
    all_to_all x1, blocking collectives, local(): lax.all_to_all(hidden.reshape(1, nodes_dev // col_devices, col_devices, h...  11.6 us
  transfers between devices with their start and end apart: 4, of which 4 were waited for; matrix products, arithmetic and copies ran while one was open for 1% of the time, Pallas kernels for 0%

commit v1 on v0

v1 whole, which is shorter than its diff:
```python
import functools

import jax
import jax.numpy as jnp
from jax import lax
from jax.experimental import pallas as pl
from jax.experimental.pallas import tpu as pltpu
from jax.sharding import PartitionSpec as P

MESH = pl.DeviceIdType.MESH


def kernel(
    R, C, Y, Z, K,
    feat, w1, b1, w2, b2, cols, cnts, tiles_hbm, out,
    tiles, panel1, panel2, scr,
    send_a1, recv_a1, send_b1, recv_b1,
    send_a2, recv_a2, send_b2, recv_b2,
    tile_sem,
    g1s, g1r, a1s, a1r, c1s, c1r,
    g2s, g2r, a2s, a2r, c2s, c2r,
):
    RB, S, B, _ = tiles.shape
    NB = panel1.shape[0] - 1
    per_chunk = RB // K
    G = max(1, 16 * C // B)
    r = lax.axis_index("row")
    c = lax.axis_index("col")
    z, y = c // Y, c % Y

    def row_peer(d):
        return (lax.rem(r + d, R), c)

    def y_peer(d):
        return (r, z * Y + lax.rem(y + d, Y))

    def z_peer(d):
        return (r, lax.rem(z + d, Z) * Y + y)

    tile_copies = []
    for k in range(K):
        rows = pl.ds(k * per_chunk, per_chunk)
        tile_copies.append(pltpu.make_async_copy(tiles_hbm.at[rows], tiles.at[rows], tile_sem.at[k]))
    for copy in tile_copies:
        copy.start()

    barrier = pltpu.get_barrier_semaphore()
    for d in range(1, R):
        pl.semaphore_signal(barrier, inc=1, device_id=row_peer(d), device_id_type=MESH)
    for d in range(1, Y):
        pl.semaphore_signal(barrier, inc=1, device_id=y_peer(d), device_id_type=MESH)
    for d in range(1, Z):
        pl.semaphore_signal(barrier, inc=1, device_id=z_peer(d), device_id_type=MESH)
    pl.semaphore_wait(barrier, R + Y + Z - 3)

    def remote(src, dst, ss, rs, peer):
        return pltpu.make_async_remote_copy(
            src_ref=src, dst_ref=dst, send_sem=ss, recv_sem=rs, device_id=peer, device_id_type=MESH
        )

    own = pl.ds(r * K, K)
    gather1 = [
        remote(feat, panel1.at[own], g1s.at[d - 1], g1r.at[d - 1], row_peer(d)) for d in range(1, R)
    ]
    for copy in gather1:
        copy.start()
    panel1[own] = feat[...]
    panel1[NB] = jnp.zeros(panel1.shape[1:], panel1.dtype)
    panel2[NB] = jnp.zeros(panel2.shape[1:], panel2.dtype)
    for copy in gather1:
        copy.wait_recv()

    def product(i, panel):
        count = cnts[i, 0]
        left, right = [], []
        for s in range(S):
            j = jnp.where(s < count, cols[i, s], NB)
            left.append(tiles[i, s])
            right.append(panel[j])
        return jnp.dot(
            jnp.concatenate(left, axis=1), jnp.concatenate(right, axis=0), preferred_element_type=jnp.float32
        )

    def compute1(k):
        tile_copies[k].wait()

        def step(t, carry):
            for g in range(G):
                scr[g * B:(g + 1) * B, :] = product(k * per_chunk + t * G + g, panel1)
            for dest in range(C):
                piece = scr[pl.ds(dest, 16, stride=C), :]
                send_a1[k, dest % Y, dest // Y, pl.ds(pl.multiple_of(t * 16, 16), 16), :] = piece.astype(jnp.bfloat16)
            return carry

        lax.fori_loop(0, per_chunk // G, step, 0)

    def compute2(k):
        def step(dest, carry):
            send_a2[k, lax.rem(dest, Y), dest // Y] = product(dest * K + k, panel2).astype(jnp.bfloat16)
            return carry

        lax.fori_loop(0, C, step, 0)

    def finish1(k, total):
        hidden = jnp.dot(total.astype(jnp.bfloat16), w1[...], preferred_element_type=jnp.float32)
        hidden = jnp.maximum(hidden + b1[...], 0.0).astype(jnp.bfloat16)
        second = jnp.dot(hidden, w2[...], preferred_element_type=jnp.float32)
        panel2[r * K + k] = second.astype(jnp.bfloat16)
        copies = []
        for d in range(1, R):
            block = panel2.at[r * K + k]
            copy = remote(block, block, g2s.at[k, d - 1], g2r.at[k, d - 1], row_peer(d))
            copy.start()
            copies.append(copy)
        return copies

    def finish2(k, total):
        out[k * B:(k + 1) * B, :] = jnp.maximum(total + b2[...], 0.0).astype(jnp.bfloat16)
        return []

    def layer(compute, finish, send_a, recv_a, send_b, recv_b, sas, sar, scs, scr_sem):
        in_a, in_b, others = {}, {}, []

        def start_a(k):
            in_a[k] = [
                remote(
                    send_a.at[k, lax.rem(y + d, Y)], recv_a.at[k, d - 1],
                    sas.at[k, d - 1], sar.at[k, d - 1], y_peer(d),
                )
                for d in range(1, Y)
            ]
            for copy in in_a[k]:
                copy.start()

        def start_b(k):
            for copy in in_a[k]:
                copy.wait_recv()
            total = send_a[k, y].astype(jnp.float32)
            for d in range(1, Y):
                total = total + recv_a[k, d - 1].astype(jnp.float32)
            send_b[k] = total.astype(jnp.bfloat16)
            in_b[k] = [
                remote(
                    send_b.at[k, lax.rem(z + d, Z)], recv_b.at[k, d - 1],
                    scs.at[k, d - 1], scr_sem.at[k, d - 1], z_peer(d),
                )
                for d in range(1, Z)
            ]
            for copy in in_b[k]:
                copy.start()

        def end(k):
            for copy in in_b[k]:
                copy.wait_recv()
            total = send_b[k, z].astype(jnp.float32)
            for d in range(1, Z):
                total = total + recv_b[k, d - 1].astype(jnp.float32)
            others.extend(finish(k, total))

        for k in range(K + 2):
            if k < K:
                compute(k)
                start_a(k)
            if 1 <= k <= K:
                start_b(k - 1)
            if k >= 2:
                end(k - 2)
        return [x for k in range(K) for x in in_a[k] + in_b[k]], others

    sent1, gather2 = layer(
        compute1, finish1, send_a1, recv_a1, send_b1, recv_b1, a1s, a1r, c1s, c1r
    )
    for copy in gather2:
        copy.wait_recv()
    sent2, _ = layer(
        compute2, finish2, send_a2, recv_a2, send_b2, recv_b2, a2s, a2r, c2s, c2r
    )
    for copy in gather1 + sent1 + gather2 + sent2:
        copy.wait_send()


def local(R, C, features, first_weight, first_bias, second_weight, second_bias, tile_values, tile_columns, tile_counts):
    nodes_dev, _, F = features.shape
    H = first_weight.shape[1]
    RB, S, B, _ = tile_values.shape
    K = nodes_dev // B
    Z = 4 if C % 4 == 0 else 1
    Y = C // Z
    NB = R * K
    G = max(1, 16 * C // B)
    bf = jnp.bfloat16
    dma = pltpu.SemaphoreType.DMA
    vmem = pl.BlockSpec(memory_space=pltpu.VMEM)
    smem = pl.BlockSpec(memory_space=pltpu.SMEM)
    ya, za, ra = max(Y - 1, 1), max(Z - 1, 1), max(R - 1, 1)
    bufs = []
    for W in (F, H):
        bufs += [
            pltpu.VMEM((K, Y, Z, B, W), bf),
            pltpu.VMEM((K, ya, Z, B, W), bf),
            pltpu.VMEM((K, Z, B, W), bf),
            pltpu.VMEM((K, za, B, W), bf),
        ]
    return pl.pallas_call(
        functools.partial(kernel, R, C, Y, Z, K),
        out_shape=jax.ShapeDtypeStruct((nodes_dev, H), bf),
        in_specs=[vmem] * 5 + [smem] * 2 + [pl.BlockSpec(memory_space=pl.ANY)],
        out_specs=vmem,
        scratch_shapes=[
            pltpu.VMEM((RB, S, B, B), bf),
            pltpu.VMEM((NB + 1, B, F), bf),
            pltpu.VMEM((NB + 1, B, H), bf),
            pltpu.VMEM((G * B, F), jnp.float32),
            *bufs,
            dma((K,)),
            dma((ra,)), dma((ra,)),
            dma((K, ya)), dma((K, ya)), dma((K, za)), dma((K, za)),
            dma((K, ra)), dma((K, ra)),
            dma((K, ya)), dma((K, ya)), dma((K, za)), dma((K, za)),
        ],
        compiler_params=pltpu.CompilerParams(
            collective_id=0, has_side_effects=True, vmem_limit_bytes=56 * 1024 * 1024
        ),
    )(
        features.reshape(K, B, F), first_weight, first_bias.reshape(1, H), second_weight,
        second_bias.reshape(1, H), tile_columns, tile_counts, tile_values,
    )


def solution(mesh):
    return jax.shard_map(
        functools.partial(local, mesh.shape["row"], mesh.shape["col"]),
        mesh=mesh,
        in_specs=(
            P("row", "col", None), P(), P(), P(), P(),
            P("row", "col", None, None), P("row", "col"), P("row", "col"),
        ),
        out_specs=P(("row", "col"), None),
        check_vma=False,
    )
```

time: 269 us -> 79 us (0.29)
  waiting for transfers between devices: 168 us -> 0 us
  Pallas kernels: 0 us -> 74.4 us
  local copies, waits for them, and re-layouts: 38 us -> 4.37 us
  matrix products: 31.7 us -> 0 us
  between operations: 13.2 us -> 0.01 us
  blocking collectives: 11.6 us -> 0 us
  other arithmetic: 4.64 us -> 0 us
    reduce_scatter x2 -> x0, waiting for transfers between devices: 136 us -> none  [local(): lax.psum_scatter(partial_value.astype(jnp.bfloat16), 'col', scatter_dimen...]
    pallas_call x0 -> x1, Pallas kernels: none -> 74.4 us  [local(): pl.pallas_call(functools.partial(kernel, R, C, Y, Z, K), out_shape=jax.Sh...]
    all_gather x2 -> x0, waiting for transfers between devices: 32.2 us -> none  [the longest x1 16.9 us: local(): lax.all_gather(scaled.reshape(nodes_dev, 1, hidden_width), 'row', axis=0,...]
    gather x8 -> x0, local copies, waits for them, and re-layouts: 31.9 us -> none  [one_group(): fetched = jnp.take(panels, columns, axis=0)]
    dot_general x10 -> x0, matrix products: 31.7 us -> none  [the longest x8 29 us: one_group(): jnp.einsum('rsik,rskf->rif', values, fetched, preferred_element_type=jnp....]
    all_to_all x1 -> x0, blocking collectives: 11.6 us -> none  [local(): lax.all_to_all(hidden.reshape(1, nodes_dev // col_devices, col_devices, h...]
  transfers between devices with their start and end apart: 4 -> 0, of which waited for: 4 -> 0; matrix products, arithmetic and copies ran while one was open for 1% -> 0% of each run, Pallas kernels for 0% -> 0%
where the time goes in v1:
time: 79 us; the launch traced here: 78.7 us
  Pallas kernels  74.4 us (94%)
  local copies, waits for them, and re-layouts  4.37 us (6%)
    pallas_call x1, Pallas kernels, local(): pl.pallas_call(functools.partial(kernel, R, C, Y, Z, K), out_shape=jax.Sh...  74.4 us
    unnamed x3, local copies, waits for them, and re-layouts  4.37 us

profile of v1, /device:TPU:0, one launch (start us, length us, event | category | flops | bytes accessed | tf_op | source)
XLA Modules:
  0.0 78.7 jit_solution(2693962305745738822)
XLA Ops:
  0.0 1.4 %copy.9.cols = s32[32,8]{1,0:T(8,128)} copy(s32[32,8]{0,1:T(8,128)} %param.14) | data formatting | bytes 2048 | tf_op args[6]
  1.4 1.3 %copy.10.cnts = s32[32,1]{1,0:T(8,128)} copy(s32[32,1]{0,1:T(1,128)} %param.15) | data formatting | bytes 256 | tf_op args[7]
  2.7 74.4 %shard_map.82 = bf16[512,256]{1,0:T(8,128)(2,1)} custom-call(bf16[4,128,128]{2,1,0:T(8,128)(2,1)} %bitcast.3, bf16[128,256]{1,0:T(8,128)(2,1)} %w1.1, f32[1,256]{1,0:T(1,128)} %bitcast.4, bf16[256,256]{1,0:T(8,128)(2,1)} %w2.1, f32[1,256]{1,0:T(1,128)} %bitcast.5, s32[32,8]{1,0:T(8,128)} %copy.9.cols, s32[32,1]{1,0:T(8,128)} %copy.10.cnts, ...), custom_call_target="tpu_custom_call" | custom-call | tf_op jit(solution)/shard_map/pallas_call | solution.py:204
  77.1 1.7 %copy.12 = bf16[512,256]{1,0:T(8,128)(2,1)} copy(bf16[512,256]{1,0:T(8,128)(2,1)} %shard_map.82) | data formatting | bytes 524288

commit v2 on v1

v2 whole, which is shorter than its diff:
```python
import functools

import jax
import jax.numpy as jnp
from jax import lax
from jax.experimental import pallas as pl
from jax.experimental.pallas import tpu as pltpu
from jax.sharding import PartitionSpec as P

MESH = pl.DeviceIdType.MESH
CHUNK = 64
LAG_A, LAG_B = 2, 4
ORDER = (2, 1, 3, 0)


def kernel(
    R, C, Y, Z, K, KB,
    feat, w1, b1, w2, b2, cols_hbm, cnts_hbm, tiles_hbm, out,
    tiles, cols, cnts, panel1, panel2, scr,
    send_a1, recv_a1, send_b1, recv_b1,
    send_a2, recv_a2, send_b2, recv_b2,
    tile_sem, index_sem,
    x1s, x1r, f1s, f1r, o1s, o1r,
    a1s, a1r, c1s, c1r,
    g2s, g2r, a2s, a2r, c2s, c2r,
):
    RB, S, B, _ = tiles.shape
    NB = panel1.shape[0] - 1
    per_chunk = RB // K
    split = B // CHUNK
    G = max(1, 16 * C // B)
    X = R // 2
    r = lax.axis_index("row")
    c = lax.axis_index("col")
    z, y = c // Y, c % Y
    x, core = r // 2, r % 2

    def row_peer(d):
        return (lax.rem(r + d, R), c)

    def y_peer(d):
        return (r, z * Y + lax.rem(y + d, Y))

    def z_peer(d):
        return (r, lax.rem(z + d, Z) * Y + y)

    def x_peer(d):
        return (lax.rem(x + d, X) * 2 + core, c)

    core_peer = (x * 2 + 1 - core, c)

    index_copies = [
        pltpu.make_async_copy(cols_hbm, cols, index_sem.at[0]),
        pltpu.make_async_copy(cnts_hbm, cnts, index_sem.at[1]),
    ]
    for copy in index_copies:
        copy.start()

    def tile_copy(k):
        rows = pl.ds(k * per_chunk, per_chunk)
        return pltpu.make_async_copy(tiles_hbm.at[rows], tiles.at[rows], tile_sem.at[k])

    barrier = pltpu.get_barrier_semaphore()
    for d in range(1, R):
        pl.semaphore_signal(barrier, inc=1, device_id=row_peer(d), device_id_type=MESH)
    for d in range(1, Y):
        pl.semaphore_signal(barrier, inc=1, device_id=y_peer(d), device_id_type=MESH)
    for d in range(1, Z):
        pl.semaphore_signal(barrier, inc=1, device_id=z_peer(d), device_id_type=MESH)
    for k in range(K):
        tile_copy(k).start()
    pl.semaphore_wait(barrier, R + Y + Z - 3)

    def remote(src, dst, ss, rs, peer):
        return pltpu.make_async_remote_copy(
            src_ref=src, dst_ref=dst, send_sem=ss, recv_sem=rs, device_id=peer, device_id_type=MESH
        )

    def blocks1(owner, h):
        return panel1.at[pl.ds(owner * KB + h * (KB // 2), KB // 2)]

    halves = [feat.at[pl.ds(h * (KB // 2), KB // 2)] for h in range(2)]
    across = {
        (h, d): remote(halves[h], blocks1(r, h), x1s.at[h, d - 1], x1r.at[h, d - 1], x_peer(d))
        for h in range(2) for d in range(1, X)
    }
    beside = [remote(halves[h], blocks1(r, h), o1s.at[h], o1r.at[h], core_peer) for h in range(2)]
    for copy in list(across.values()) + beside:
        copy.start()
    panel1[pl.ds(r * KB, KB)] = feat[...]
    panel1[NB] = jnp.zeros(panel1.shape[1:], panel1.dtype)
    panel2[NB] = jnp.zeros(panel2.shape[1:], panel2.dtype)
    onward = []
    for (h, d), copy in across.items():
        copy.wait_recv()
        block = blocks1(lax.rem(x - d + X, X) * 2 + core, h)
        ahead = remote(block, block, f1s.at[h, d - 1], f1r.at[h, d - 1], core_peer)
        ahead.start()
        onward.append(ahead)
    for copy in beside + onward:
        copy.wait_recv()
    for copy in index_copies:
        copy.wait()

    def product(i, panel):
        count = cnts[0, i]
        left, right = [], []
        for s in range(S):
            j = jnp.where(s < count, cols[s, i], NB)
            left.append(tiles[i, s])
            right.append(panel[j])
        return jnp.dot(
            jnp.concatenate(left, axis=1), jnp.concatenate(right, axis=0), preferred_element_type=jnp.float32
        )

    class Sums:
        def __init__(self, bufs, sems, width):
            self.send_a, self.recv_a, self.send_b, self.recv_b = bufs
            self.sas, self.sar, self.sbs, self.sbr = sems
            self.width = width

        def copies_a(self, k, p):
            part = pl.ds(p * self.width, self.width)
            return [
                remote(
                    self.send_a.at[k, lax.rem(y + e, Y), part], self.recv_a.at[k, e - 1, part],
                    self.sas.at[k, p, e - 1], self.sar.at[k, p, e - 1], y_peer(e),
                )
                for e in range(1, Y)
            ]

        def copy_b(self, k, d):
            return remote(
                self.send_b.at[k, d - 1], self.recv_b.at[k, d - 1],
                self.sbs.at[k, d - 1], self.sbr.at[k, d - 1], z_peer(d),
            )

        def start_a(self, k, p):
            for copy in self.copies_a(k, p):
                copy.start()

        def pair_sum(self, k, d):
            total = self.send_a[k, y, d].astype(jnp.float32)
            for e in range(1, Y):
                total = total + self.recv_a[k, e - 1, d].astype(jnp.float32)
            return total

        def start_b(self, k, p):
            for copy in self.copies_a(k, p):
                copy.wait_recv()
            for d in ORDER:
                if d > 0 and d // self.width == p:
                    self.send_b[k, d - 1] = self.pair_sum(k, d).astype(jnp.bfloat16)
                    self.copy_b(k, d).start()

        def end(self, k):
            total = self.pair_sum(k, 0)
            for d in range(1, Z):
                self.copy_b(k, d).wait_recv()
                total = total + self.recv_b[k, d - 1].astype(jnp.float32)
            return total

        def wait_sends(self, k):
            for p in range(Z // self.width):
                for copy in self.copies_a(k, p):
                    copy.wait_send()
            for d in range(1, Z):
                self.copy_b(k, d).wait_send()

    sums1 = Sums((send_a1, recv_a1, send_b1, recv_b1), (a1s, a1r, c1s, c1r), Z)
    sums2 = Sums((send_a2, recv_a2, send_b2, recv_b2), (a2s, a2r, c2s, c2r), 1)

    def gather2(k):
        block = panel2.at[r * KB + k // split, pl.ds(pl.multiple_of(k % split * CHUNK, CHUNK), CHUNK)]
        return [remote(block, block, g2s.at[k, d - 1], g2r.at[k, d - 1], row_peer(d)) for d in range(1, R)]

    def layer1(k, carry):
        @pl.when(k < K)
        def _():
            tile_copy(k).wait()

            def step(t, inner):
                for g in range(G):
                    scr[g * B:(g + 1) * B, :] = product(k * per_chunk + t * G + g, panel1)
                for dest in range(C):
                    piece = scr[pl.ds(dest, 16, stride=C), :].astype(jnp.bfloat16)
                    d = lax.rem(dest // Y - z + Z, Z)
                    send_a1[k, dest % Y, d, pl.ds(pl.multiple_of(t * 16, 16), 16), :] = piece
                return inner

            lax.fori_loop(0, per_chunk // G, step, 0)
            sums1.start_a(k, 0)

        @pl.when((k >= LAG_A) & (k < K + LAG_A))
        def _():
            sums1.start_b(k - LAG_A, 0)

        @pl.when(k >= LAG_B)
        def _():
            n = k - LAG_B
            total = sums1.end(n).astype(jnp.bfloat16)
            hidden = jnp.dot(total, w1[...], preferred_element_type=jnp.float32)
            hidden = jnp.maximum(hidden + b1[...], 0.0).astype(jnp.bfloat16)
            second = jnp.dot(hidden, w2[...], preferred_element_type=jnp.float32).astype(jnp.bfloat16)
            panel2[r * KB + n // split, pl.ds(pl.multiple_of(n % split * CHUNK, CHUNK), CHUNK), :] = second
            for copy in gather2(n):
                copy.start()

        return carry

    lax.fori_loop(0, K + LAG_B, layer1, 0)

    def arrive(k, carry):
        for copy in gather2(k):
            copy.wait_recv()
        return carry

    lax.fori_loop(0, K, arrive, 0)

    def layer2(k, carry):
        for d in ORDER:
            if d >= Z:
                continue

            @pl.when(k < KB)
            def _():
                for e in list(range(1, Y)) + [0]:
                    to = lax.rem(y + e, Y)
                    dest = lax.rem(z + d, Z) * Y + to
                    send_a2[k, to, d] = product(dest * KB + k, panel2).astype(jnp.bfloat16)
                    if e == Y - 1:
                        sums2.start_a(k, d)

            @pl.when((k >= 1) & (k <= KB))
            def _():
                sums2.start_b(k - 1, d)

        @pl.when(k >= 2)
        def _():
            n = k - 2
            total = jnp.maximum(sums2.end(n) + b2[...], 0.0)
            out[pl.ds(pl.multiple_of(n * B, B), B), :] = total.astype(jnp.bfloat16)

        return carry

    lax.fori_loop(0, KB + 2, layer2, 0)

    for copy in list(across.values()) + beside + onward:
        copy.wait_send()

    def sent1(k, carry):
        sums1.wait_sends(k)
        for copy in gather2(k):
            copy.wait_send()
        return carry

    def sent2(k, carry):
        sums2.wait_sends(k)
        return carry

    lax.fori_loop(0, K, sent1, 0)
    lax.fori_loop(0, KB, sent2, 0)


def local(R, C, features, first_weight, first_bias, second_weight, second_bias, tile_values, tile_columns, tile_counts):
    nodes_dev, _, F = features.shape
    H = first_weight.shape[1]
    RB, S, B, _ = tile_values.shape
    K = nodes_dev // CHUNK
    KB = nodes_dev // B
    Z = 4
    Y = C // Z
    X = R // 2
    NB = R * KB
    G = max(1, 16 * C // B)
    bf = jnp.bfloat16
    dma = pltpu.SemaphoreType.DMA
    vmem = pl.BlockSpec(memory_space=pltpu.VMEM)
    hbm = pl.BlockSpec(memory_space=pl.ANY)
    bufs = []
    for n, rows, W in ((K, CHUNK, F), (KB, B, H)):
        bufs += [
            pltpu.VMEM((n, Y, Z, rows, W), bf),
            pltpu.VMEM((n, Y - 1, Z, rows, W), bf),
            pltpu.VMEM((n, Z - 1, rows, W), bf),
            pltpu.VMEM((n, Z - 1, rows, W), bf),
        ]
    return pl.pallas_call(
        functools.partial(kernel, R, C, Y, Z, K, KB),
        out_shape=jax.ShapeDtypeStruct((nodes_dev, H), bf),
        in_specs=[vmem] * 5 + [hbm] * 3,
        out_specs=vmem,
        scratch_shapes=[
            pltpu.VMEM((RB, S, B, B), bf),
            pltpu.SMEM((S, RB), jnp.int32),
            pltpu.SMEM((1, RB), jnp.int32),
            pltpu.VMEM((NB + 1, B, F), bf),
            pltpu.VMEM((NB + 1, B, H), bf),
            pltpu.VMEM((G * B, F), jnp.float32),
            *bufs,
            dma((K,)), dma((2,)),
            dma((2, X - 1)), dma((2, X - 1)), dma((2, X - 1)), dma((2, X - 1)), dma((2,)), dma((2,)),
            dma((K, 1, Y - 1)), dma((K, 1, Y - 1)), dma((K, Z - 1)), dma((K, Z - 1)),
            dma((K, R - 1)), dma((K, R - 1)),
            dma((KB, Z, Y - 1)), dma((KB, Z, Y - 1)), dma((KB, Z - 1)), dma((KB, Z - 1)),
        ],
        compiler_params=pltpu.CompilerParams(
            collective_id=0, has_side_effects=True, vmem_limit_bytes=56 * 1024 * 1024
        ),
    )(
        features.reshape(KB, B, F), first_weight, first_bias.reshape(1, H), second_weight,
        second_bias.reshape(1, H), tile_columns.T, tile_counts.T, tile_values,
    )


def solution(mesh):
    return jax.shard_map(
        functools.partial(local, mesh.shape["row"], mesh.shape["col"]),
        mesh=mesh,
        in_specs=(
            P("row", "col", None), P(), P(), P(), P(),
            P("row", "col", None, None), P("row", "col"), P("row", "col"),
        ),
        out_specs=P(("row", "col"), None),
        check_vma=False,
    )
```

time: 79 us -> 66.3 us (0.84)
  Pallas kernels: 74.4 us -> 64.5 us
  local copies, waits for them, and re-layouts: 4.37 us -> 1.67 us
    pallas_call x1, Pallas kernels: 74.4 us -> 64.5 us  [local(): pl.pallas_call(functools.partial(kernel, R, C, Y, Z, K, KB), out_shape=ja...]
    unnamed x3 -> x1, local copies, waits for them, and re-layouts: 4.37 us -> 1.67 us
where the time goes in v2:
time: 66.3 us; the launch traced here: 66.2 us
  Pallas kernels  64.5 us (97%)
  local copies, waits for them, and re-layouts  1.67 us (3%)
    pallas_call x1, Pallas kernels, local(): pl.pallas_call(functools.partial(kernel, R, C, Y, Z, K, KB), out_shape=ja...  64.5 us
    unnamed x1, local copies, waits for them, and re-layouts  1.67 us

profile of v2, /device:TPU:0, one launch (start us, length us, event | category | flops | bytes accessed | tf_op | source)
XLA Modules:
  0.0 66.2 jit_solution(17994087822800085138)
XLA Ops:
  0.0 64.5 %shard_map.82 = bf16[512,256]{1,0:T(8,128)(2,1)} custom-call(bf16[4,128,128]{2,1,0:T(8,128)(2,1)} %bitcast.5, bf16[128,256]{1,0:T(8,128)(2,1)} %w1.1, f32[1,256]{1,0:T(1,128)} %bitcast.7, bf16[256,256]{1,0:T(8,128)(2,1)} %w2.1, f32[1,256]{1,0:T(1,128)} %bitcast.8, s32[8,32]{1,0:T(8,128)} %bitcast.6, s32[1,32]{1,0:T(1,128)} %bitcast.9, ...), custom_call_target="tpu_custom_call" | custom-call | tf_op jit(solution)/shard_map/pallas_call | solution.py:288
  64.5 1.7 %copy.10 = bf16[512,256]{1,0:T(8,128)(2,1)} copy(bf16[512,256]{1,0:T(8,128)(2,1)} %shard_map.82) | data formatting | bytes 524288

commit v3 on v2

--- a/solution.py
+++ b/solution.py
@@ -9,20 +9,20 @@
 
 MESH = pl.DeviceIdType.MESH
 CHUNK = 64
-LAG_A, LAG_B = 2, 4
+LAG_A, LAG_B = 2, 3
 ORDER = (2, 1, 3, 0)
 
 
 def kernel(
     R, C, Y, Z, K, KB,
-    feat, w1, b1, w2, b2, cols_hbm, cnts_hbm, tiles_hbm, out,
-    tiles, cols, cnts, panel1, panel2, scr,
+    feat, w1_hbm, b1_hbm, w2_hbm, b2_hbm, cols_hbm, cnts_hbm, tiles_hbm, out_hbm,
+    w1, b1, w2, b2, out, tiles, cols, cnts, panel1, panel2, scr,
     send_a1, recv_a1, send_b1, recv_b1,
     send_a2, recv_a2, send_b2, recv_b2,
-    tile_sem, index_sem,
+    tile_sem, local_sem, out_sem,
     x1s, x1r, f1s, f1r, o1s, o1r,
     a1s, a1r, c1s, c1r,
-    g2s, g2r, a2s, a2r, c2s, c2r,
+    g2s, g2r, f2s, f2r, a2s, a2r, c2s, c2r,
 ):
     RB, S, B, _ = tiles.shape
     NB = panel1.shape[0] - 1
@@ -49,13 +49,6 @@
 
     core_peer = (x * 2 + 1 - core, c)
 
-    index_copies = [
-        pltpu.make_async_copy(cols_hbm, cols, index_sem.at[0]),
-        pltpu.make_async_copy(cnts_hbm, cnts, index_sem.at[1]),
-    ]
-    for copy in index_copies:
-        copy.start()
-
     def tile_copy(k):
         rows = pl.ds(k * per_chunk, per_chunk)
         return pltpu.make_async_copy(tiles_hbm.at[rows], tiles.at[rows], tile_sem.at[k])
@@ -67,8 +60,18 @@
         pl.semaphore_signal(barrier, inc=1, device_id=y_peer(d), device_id_type=MESH)
     for d in range(1, Z):
         pl.semaphore_signal(barrier, inc=1, device_id=z_peer(d), device_id_type=MESH)
+    own = pl.ds(r * KB, KB)
+    pairs = [
+        (feat, panel1.at[own]), (cols_hbm, cols), (cnts_hbm, cnts),
+        (w1_hbm, w1), (b1_hbm, b1), (w2_hbm, w2), (b2_hbm, b2),
+    ]
+    local_copies = [pltpu.make_async_copy(a, b, local_sem.at[n]) for n, (a, b) in enumerate(pairs)]
+    for copy in local_copies:
+        copy.start()
     for k in range(K):
         tile_copy(k).start()
+    panel1[NB] = jnp.zeros(panel1.shape[1:], panel1.dtype)
+    panel2[NB] = jnp.zeros(panel2.shape[1:], panel2.dtype)
     pl.semaphore_wait(barrier, R + Y + Z - 3)
 
     def remote(src, dst, ss, rs, peer):
@@ -87,9 +90,6 @@
     beside = [remote(halves[h], blocks1(r, h), o1s.at[h], o1r.at[h], core_peer) for h in range(2)]
     for copy in list(across.values()) + beside:
         copy.start()
-    panel1[pl.ds(r * KB, KB)] = feat[...]
-    panel1[NB] = jnp.zeros(panel1.shape[1:], panel1.dtype)
-    panel2[NB] = jnp.zeros(panel2.shape[1:], panel2.dtype)
     onward = []
     for (h, d), copy in across.items():
         copy.wait_recv()
@@ -99,7 +99,7 @@
         onward.append(ahead)
     for copy in beside + onward:
         copy.wait_recv()
-    for copy in index_copies:
+    for copy in local_copies:
         copy.wait()
 
     def product(i, panel):
@@ -170,9 +170,27 @@
     sums1 = Sums((send_a1, recv_a1, send_b1, recv_b1), (a1s, a1r, c1s, c1r), Z)
     sums2 = Sums((send_a2, recv_a2, send_b2, recv_b2), (a2s, a2r, c2s, c2r), 1)
 
-    def gather2(k):
-        block = panel2.at[r * KB + k // split, pl.ds(pl.multiple_of(k % split * CHUNK, CHUNK), CHUNK)]
-        return [remote(block, block, g2s.at[k, d - 1], g2r.at[k, d - 1], row_peer(d)) for d in range(1, R)]
+    def block2(owner, k):
+        return panel2.at[owner * KB + k // split, pl.ds(pl.multiple_of(k % split * CHUNK, CHUNK), CHUNK)]
+
+    def beside2(k):
+        return [remote(block2(r, k), block2(r, k), g2s.at[k, 0], g2r.at[k, 0], core_peer)]
+
+    def across2(k):
+        block = block2(r, k)
+        return [remote(block, block, g2s.at[k, d], g2r.at[k, d], x_peer(d)) for d in range(1, X)]
+
+    def onward2(k):
+        blocks = [block2(lax.rem(x - d + X, X) * 2 + core, k) for d in range(1, X)]
+        return [
+            remote(block, block, f2s.at[k, d], f2r.at[k, d], core_peer) for d, block in enumerate(blocks)
+        ]
+
+    def forward2(k):
+        for copy in across2(k):
+            copy.wait_recv()
+        for copy in onward2(k):
+            copy.start()
 
     def layer1(k, carry):
         @pl.when(k < K)
@@ -203,19 +221,28 @@
             hidden = jnp.maximum(hidden + b1[...], 0.0).astype(jnp.bfloat16)
             second = jnp.dot(hidden, w2[...], preferred_element_type=jnp.float32).astype(jnp.bfloat16)
             panel2[r * KB + n // split, pl.ds(pl.multiple_of(n % split * CHUNK, CHUNK), CHUNK), :] = second
-            for copy in gather2(n):
+            for copy in across2(n) + beside2(n):
                 copy.start()
 
+        @pl.when(k >= LAG_B + 1)
+        def _():
+            forward2(k - LAG_B - 1)
+
         return carry
 
     lax.fori_loop(0, K + LAG_B, layer1, 0)
+    forward2(K - 1)
 
     def arrive(k, carry):
-        for copy in gather2(k):
+        for copy in beside2(k) + onward2(k):
             copy.wait_recv()
         return carry
 
     lax.fori_loop(0, K, arrive, 0)
+
+    def out_copy(n):
+        rows = pl.ds(pl.multiple_of(n * B, B), B)
+        return pltpu.make_async_copy(out.at[rows], out_hbm.at[rows], out_sem.at[n])
 
     def layer2(k, carry):
         for d in ORDER:
@@ -240,6 +267,7 @@
             n = k - 2
             total = jnp.maximum(sums2.end(n) + b2[...], 0.0)
             out[pl.ds(pl.multiple_of(n * B, B), B), :] = total.astype(jnp.bfloat16)
+            out_copy(n).start()
 
         return carry
 
@@ -250,12 +278,13 @@
 
     def sent1(k, carry):
         sums1.wait_sends(k)
-        for copy in gather2(k):
+        for copy in across2(k) + beside2(k) + onward2(k):
             copy.wait_send()
         return carry
 
     def sent2(k, carry):
         sums2.wait_sends(k)
+        out_copy(k).wait()
         return carry
 
     lax.fori_loop(0, K, sent1, 0)
@@ -275,7 +304,6 @@
     G = max(1, 16 * C // B)
     bf = jnp.bfloat16
     dma = pltpu.SemaphoreType.DMA
-    vmem = pl.BlockSpec(memory_space=pltpu.VMEM)
     hbm = pl.BlockSpec(memory_space=pl.ANY)
     bufs = []
     for n, rows, W in ((K, CHUNK, F), (KB, B, H)):
@@ -288,9 +316,14 @@
     return pl.pallas_call(
         functools.partial(kernel, R, C, Y, Z, K, KB),
         out_shape=jax.ShapeDtypeStruct((nodes_dev, H), bf),
-        in_specs=[vmem] * 5 + [hbm] * 3,
-        out_specs=vmem,
+        in_specs=[hbm] * 8,
+        out_specs=hbm,
         scratch_shapes=[
+            pltpu.VMEM((F, H), bf),
+            pltpu.VMEM((1, H), jnp.float32),
+            pltpu.VMEM((H, H), bf),
+            pltpu.VMEM((1, H), jnp.float32),
+            pltpu.VMEM((nodes_dev, H), bf),
             pltpu.VMEM((RB, S, B, B), bf),
             pltpu.SMEM((S, RB), jnp.int32),
             pltpu.SMEM((1, RB), jnp.int32),
@@ -298,10 +331,10 @@
             pltpu.VMEM((NB + 1, B, H), bf),
             pltpu.VMEM((G * B, F), jnp.float32),
             *bufs,
-            dma((K,)), dma((2,)),
+            dma((K,)), dma((7,)), dma((KB,)),
             dma((2, X - 1)), dma((2, X - 1)), dma((2, X - 1)), dma((2, X - 1)), dma((2,)), dma((2,)),
             dma((K, 1, Y - 1)), dma((K, 1, Y - 1)), dma((K, Z - 1)), dma((K, Z - 1)),
-            dma((K, R - 1)), dma((K, R - 1)),
+            dma((K, X)), dma((K, X)), dma((K, X - 1)), dma((K, X - 1)),
             dma((KB, Z, Y - 1)), dma((KB, Z, Y - 1)), dma((KB, Z - 1)), dma((KB, Z - 1)),
         ],
         compiler_params=pltpu.CompilerParams(

time: 66.3 us -> 72 us (1.086)
  Pallas kernels: 64.5 us -> 70.2 us
    pallas_call x1, Pallas kernels: 64.5 us -> 70.2 us  [local(): pl.pallas_call(functools.partial(kernel, R, C, Y, Z, K, KB), out_shape=ja...]
where the time goes in v3:
time: 72 us; the launch traced here: 71.9 us
  Pallas kernels  70.2 us (98%)
  local copies, waits for them, and re-layouts  1.67 us (2%)
    pallas_call x1, Pallas kernels, local(): pl.pallas_call(functools.partial(kernel, R, C, Y, Z, K, KB), out_shape=ja...  70.2 us
    unnamed x1, local copies, waits for them, and re-layouts  1.67 us

profile of v3, /device:TPU:0, one launch (start us, length us, event | category | flops | bytes accessed | tf_op | source)
XLA Modules:
  0.0 71.9 jit_solution(4566833252087221674)
XLA Ops:
  0.0 70.2 %shard_map.82 = bf16[512,256]{1,0:T(8,128)(2,1)} custom-call(bf16[4,128,128]{2,1,0:T(8,128)(2,1)} %bitcast.5, bf16[128,256]{1,0:T(8,128)(2,1)} %w1_hbm.1, f32[1,256]{1,0:T(1,128)} %bitcast.7, bf16[256,256]{1,0:T(8,128)(2,1)} %w2_hbm.1, f32[1,256]{1,0:T(1,128)} %bitcast.8, s32[8,32]{1,0:T(8,128)} %bitcast.6, s32[1,32]{1,0:T(1,128)} %bitcast.9, ...), custom_call_target="tpu_custom_call" | custom-call | tf_op jit(solution)/shard_map/pallas_call | solution.py:316
  70.2 1.7 %copy.10 = bf16[512,256]{1,0:T(8,128)(2,1)} copy(bf16[512,256]{1,0:T(8,128)(2,1)} %shard_map.82) | data formatting | bytes 524288

commit v4 on v3

--- a/solution.py
+++ b/solution.py
@@ -9,7 +9,7 @@
 
 MESH = pl.DeviceIdType.MESH
 CHUNK = 64
-LAG_A, LAG_B = 2, 3
+LAG_A, LAG_B = 3, 6
 ORDER = (2, 1, 3, 0)
 
 
@@ -68,8 +68,6 @@
     local_copies = [pltpu.make_async_copy(a, b, local_sem.at[n]) for n, (a, b) in enumerate(pairs)]
     for copy in local_copies:
         copy.start()
-    for k in range(K):
-        tile_copy(k).start()
     panel1[NB] = jnp.zeros(panel1.shape[1:], panel1.dtype)
     panel2[NB] = jnp.zeros(panel2.shape[1:], panel2.dtype)
     pl.semaphore_wait(barrier, R + Y + Z - 3)
@@ -90,6 +88,8 @@
     beside = [remote(halves[h], blocks1(r, h), o1s.at[h], o1r.at[h], core_peer) for h in range(2)]
     for copy in list(across.values()) + beside:
         copy.start()
+    for k in range(K):
+        tile_copy(k).start()
     onward = []
     for (h, d), copy in across.items():
         copy.wait_recv()
@@ -224,14 +224,16 @@
             for copy in across2(n) + beside2(n):
                 copy.start()
 
-        @pl.when(k >= LAG_B + 1)
-        def _():
-            forward2(k - LAG_B - 1)
 
         return carry
 
     lax.fori_loop(0, K + LAG_B, layer1, 0)
-    forward2(K - 1)
+
+    def forward(k, carry):
+        forward2(k)
+        return carry
+
+    lax.fori_loop(0, K, forward, 0)
 
     def arrive(k, carry):
         for copy in beside2(k) + onward2(k):

time: 72 us -> 64.6 us (0.90)
  Pallas kernels: 70.2 us -> 62.8 us
    pallas_call x1, Pallas kernels: 70.2 us -> 62.8 us  [local(): pl.pallas_call(functools.partial(kernel, R, C, Y, Z, K, KB), out_shape=ja...]
where the time goes in v4:
time: 64.6 us; the launch traced here: 64.5 us
  Pallas kernels  62.8 us (97%)
  local copies, waits for them, and re-layouts  1.67 us (3%)
    pallas_call x1, Pallas kernels, local(): pl.pallas_call(functools.partial(kernel, R, C, Y, Z, K, KB), out_shape=ja...  62.8 us
    unnamed x1, local copies, waits for them, and re-layouts  1.67 us

profile of v4, /device:TPU:0, one launch (start us, length us, event | category | flops | bytes accessed | tf_op | source)
XLA Modules:
  0.0 64.5 jit_solution(11923870405536394946)
XLA Ops:
  0.0 62.8 %shard_map.82 = bf16[512,256]{1,0:T(8,128)(2,1)} custom-call(bf16[4,128,128]{2,1,0:T(8,128)(2,1)} %bitcast.5, bf16[128,256]{1,0:T(8,128)(2,1)} %w1_hbm.1, f32[1,256]{1,0:T(1,128)} %bitcast.7, bf16[256,256]{1,0:T(8,128)(2,1)} %w2_hbm.1, f32[1,256]{1,0:T(1,128)} %bitcast.8, s32[8,32]{1,0:T(8,128)} %bitcast.6, s32[1,32]{1,0:T(1,128)} %bitcast.9, ...), custom_call_target="tpu_custom_call" | custom-call | tf_op jit(solution)/shard_map/pallas_call | solution.py:318
  62.8 1.7 %copy.10 = bf16[512,256]{1,0:T(8,128)(2,1)} copy(bf16[512,256]{1,0:T(8,128)(2,1)} %shard_map.82) | data formatting | bytes 524288
